TPU v7x, 256 devices: a whole 4x4x8 slice. The times are simulated.
256 devices in a mesh: ctx: 64 (over y_hi, x, z), grp: 4 (over y_lo, core).
Axes of the slice: x: 4, y: 4 (y_hi: 2, y_lo: 2; y = y_hi * 2 + y_lo), z: 8, core: 2. Of those that a mesh axis runs over, the one named last changes fastest.
Arguments:
- queries: bfloat16 [32768, 4096], P('ctx', 'grp'), parts along dimension 1, may hold values from -6 to 6
- keys: bfloat16 [32768, 512], P('ctx', 'grp'), parts along dimension 1, may hold values from -6 to 6
- values: bfloat16 [32768, 512], P('ctx', 'grp'), parts along dimension 1, may hold values from -6 to 6
- outputs: bfloat16 [32768, 4096], P('ctx', 'grp'), parts along dimension 1, may hold values from -6 to 6
- out_grad: bfloat16 [32768, 4096], P('ctx', 'grp'), parts along dimension 1, may hold values from -6 to 6
- log_sums: float32 [32, 32768], P('grp', 'ctx'), parts along dimension 0, may hold values from 3 to 6
- pair_of: int32 [64], replicated, may hold values from 0 to 63, each once
Outputs:
- grad_queries: bfloat16 [32768, 4096], P('ctx', 'grp'), parts along dimension 1
- grad_keys: float32 [32768, 512], P('ctx', 'grp'), parts along dimension 1
- grad_values: float32 [32768, 512], P('ctx', 'grp'), parts along dimension 1
There are 4 independent parts, one for each index of `grp`. A program takes and returns all parts, laid end to end along the dimension named above; an argument that names none is the same for every part. Nothing has to cross between parts.
Inputs may be any that keep to these rules, and one draw needn't show every extreme that they name: Each value appears once; device d holds the segments pair_of[d] and 127 - pair_of[d], each of 256 tokens.
All inputs are finite; a program needn't handle non-finite values.
Results may differ from a plain program's by a relative error of at most 0.0058.
Values may be sent and summed in bfloat16 or wider, within the bound.
A program may use at most 128 MiB of HBM per device.

v0:
```python
import jax
import jax.numpy as jnp
from jax import lax
from jax.experimental import pallas as pl
from jax.experimental.pallas import tpu as pltpu
from jax.sharding import PartitionSpec as P

MESH = pl.DeviceIdType.MESH
LOG2E = 1.4426950408889634
SEG = 256
HEADS = 8
DIM = 128
ROWS = HEADS * SEG
FACTOR = DIM**-0.5


def dot_nt(a, b):
    return lax.dot_general(a, b, (((1,), (1,)), ((), ())), preferred_element_type=jnp.float32)


def dot_nn(a, b):
    return lax.dot_general(a, b, (((1,), (0,)), ((), ())), preferred_element_type=jnp.float32)


def kernel(
    ctx_count,
    pair_ref, q_hbm, k_ref, v_ref, o_hbm, g_hbm, lse_ref,
    dq_hbm, dk_ref, dv_ref,
    q_in, g_in, o_in,
    q_t, g_t, lse_b, delta_b,
    k1, k2, k3, v1, v2, v3,
    probs, dsc,
    dq_acc, dq_out, own_v, own_k, sent_v, sent_k, got_v, got_k,
    in_sem, out_sem,
    k_send, k_recv, v_send, v_recv, gv_send, gv_recv, gk_send, gk_recv,
):
    me = lax.axis_index("ctx")
    right = lax.rem(me + 1, ctx_count)
    left = lax.rem(me + ctx_count - 1, ctx_count)

    barrier = pltpu.get_barrier_semaphore()
    for peer in (left, right):
        pl.semaphore_signal(barrier, inc=1, device_id={"ctx": peer}, device_id_type=MESH)

    loads = []
    for i, (src, dst) in enumerate(((q_hbm, q_in), (g_hbm, g_in), (o_hbm, o_in))):
        for sg in range(2):
            load = pltpu.make_async_copy(src.at[pl.ds(sg * SEG, SEG)], dst.at[sg], in_sem.at[i, sg])
            load.start()
            loads.append(load)

    keys = [None, k1, k2, k3]
    values = [None, v1, v2, v3]

    def forward(bufs, first, step, seg, send, recv):
        src = first.at[pl.ds(seg * SEG, SEG)] if step == 0 else bufs[step].at[seg]
        return pltpu.make_async_remote_copy(
            src_ref=src,
            dst_ref=bufs[step + 1].at[seg],
            send_sem=send.at[step, seg],
            recv_sem=recv.at[step, seg],
            device_id={"ctx": right},
            device_id_type=MESH,
        )

    key_copy = [[forward(keys, k_ref, s, g, k_send, k_recv) for g in range(2)] for s in range(3)]
    value_copy = [[forward(values, v_ref, s, g, v_send, v_recv) for g in range(2)] for s in range(3)]

    def back(sent, got, step, seg, send, recv):
        return pltpu.make_async_remote_copy(
            src_ref=sent.at[step - 1, seg],
            dst_ref=got.at[step - 1, seg],
            send_sem=send.at[step - 1, seg],
            recv_sem=recv.at[step - 1, seg],
            device_id={"ctx": left},
            device_id_type=MESH,
        )

    gv_copy = [None] + [[back(sent_v, got_v, s, g, gv_send, gv_recv) for g in range(2)] for s in (1, 2, 3)]
    gk_copy = [None] + [[back(sent_k, got_k, s, g, gk_send, gk_recv) for g in range(2)] for s in (1, 2, 3)]

    pl.semaphore_wait(barrier, 2)
    key_copy[0][0].start()
    key_copy[0][1].start()
    value_copy[0][0].start()

    for load in loads:
        load.wait()
    for h in range(HEADS):
        cols = slice(h * DIM, (h + 1) * DIM)
        for sg in range(2):
            qh = q_in[sg, :, cols]
            gh = g_in[sg, :, cols]
            q_t[sg, :, h * SEG : (h + 1) * SEG] = qh.T
            g_t[sg, :, h * SEG : (h + 1) * SEG] = gh.T
            delta = jnp.sum(
                gh.astype(jnp.float32) * o_in[sg, :, cols].astype(jnp.float32), axis=1, keepdims=True
            )
            delta_b[sg, h * SEG : (h + 1) * SEG, :] = jnp.broadcast_to(delta, (SEG, DIM))
            for j in range(SEG // DIM):
                at = sg * SEG + j * DIM
                row = lse_ref[h : h + 1, at : at + DIM] * LOG2E
                lse_b[sg, h * SEG + j * DIM : h * SEG + (j + 1) * DIM, :] = jnp.broadcast_to(row, (DIM, DIM)).T

    def wide(x):
        return jnp.concatenate([x, x], axis=1)

    def probs_of(q_seg, key, out, diagonal):
        for h in range(HEADS):
            rows = pl.ds(h * SEG, SEG)
            qh = q_heads(q_seg, h)
            x = dot_nt(qh, key) * (FACTOR * LOG2E) - wide(lse_b[q_seg, rows, :])
            p = jnp.exp2(x)
            if diagonal:
                below = lax.broadcasted_iota(jnp.int32, (SEG, SEG), 1) <= lax.broadcasted_iota(
                    jnp.int32, (SEG, SEG), 0
                )
                p = jnp.where(below, p, 0.0)
            out[rows, :] = p.astype(jnp.bfloat16)

    def dscores_of(q_seg, value, pin, out):
        for h in range(HEADS):
            rows = pl.ds(h * SEG, SEG)
            dp = dot_nt(g_heads(q_seg, h), value)
            ds = pin[rows, :].astype(jnp.float32) * (dp - wide(delta_b[q_seg, rows, :]))
            out[rows, :] = ds.astype(jnp.bfloat16)

    def q_heads(q_seg, h):
        return q_in[q_seg, :, h * DIM : (h + 1) * DIM]

    def g_heads(q_seg, h):
        return g_in[q_seg, :, h * DIM : (h + 1) * DIM]

    def own_tile(q_seg, k_seg, diagonal, first_q, first_k):
        key = k_ref[k_seg * SEG : (k_seg + 1) * SEG, :]
        value = v_ref[k_seg * SEG : (k_seg + 1) * SEG, :]
        p, d = probs.at[0, 0], dsc.at[0]
        probs_of(q_seg, key, p, diagonal)
        dscores_of(q_seg, value, p, d)
        part_v = dot_nn(g_t[q_seg], p[...])
        part_k = dot_nn(q_t[q_seg], d[...])
        part_q = dot_nn(d[...], key)
        if first_k:
            own_v[0, k_seg] = part_v
            own_k[0, k_seg] = part_k
        else:
            own_v[0, k_seg] += part_v
            own_k[0, k_seg] += part_k
        if first_q:
            dq_acc[q_seg] = part_q
        else:
            dq_acc[q_seg] += part_q

    mine = pair_ref[me]
    b_seg = [None] + [
        lax.div(pair_ref[lax.rem(me + ctx_count - s, ctx_count)] - mine + ctx_count, ctx_count) for s in (1, 2, 3)
    ]

    def pick(step, earlier, later):
        return jnp.where(jnp.broadcast_to(b_seg[step], earlier.shape) == 0, earlier, later)

    def spread(own, step, part_a, part_b):
        zero = jnp.zeros_like(part_b)
        own[step, 0] = part_a + pick(step, part_b, zero)
        own[step, 1] = pick(step, zero, part_b)

    def stage_v(s):
        qb = b_seg[s]
        key_a = keys[s][0]
        key_b = pick(s, key_a, keys[s][1])
        probs_of(1, key_a, probs.at[s, 0], False)
        probs_of(qb, key_b, probs.at[s, 1], False)
        spread(own_v, s, dot_nn(g_t[1], probs[s, 0]), dot_nn(g_t[qb], probs[s, 1]))

    def stage_k(s):
        qb = b_seg[s]
        key_a = keys[s][0]
        key_b = pick(s, key_a, keys[s][1])
        value_a = values[s][0]
        value_b = pick(s, value_a, values[s][1])
        dscores_of(1, value_a, probs.at[s, 0], dsc.at[0])
        dscores_of(qb, value_b, probs.at[s, 1], dsc.at[1])
        spread(own_k, s, dot_nn(q_t[1], dsc[0]), dot_nn(q_t[qb], dsc[1]))

        def rest():
            part_b = dot_nn(dsc[1], key_b)
            zero = jnp.zeros_like(part_b)
            dq_acc[1] += dot_nn(dsc[0], key_a) + pick(s, zero, part_b)
            dq_acc[0] += pick(s, part_b, zero)

        return rest

    def pass_back(copies, own, sent, got, s, seg):
        total = own[s, seg]
        if s < 3:
            copies[s + 1][seg].wait_recv()
            total = total + got[s, seg].astype(jnp.float32)
        sent[s - 1, seg] = total.astype(jnp.bfloat16)
        copies[s][seg].start()

    def finish(copies, own, got, seg, scale, out):
        copies[1][seg].wait_recv()
        total = own[0, seg] + got[0, seg].astype(jnp.float32)
        if scale is not None:
            total = total * scale
        out[seg * SEG : (seg + 1) * SEG, :] = total.T

    def arrived(copies, step, seg):
        copies[step - 1][seg].wait_recv()
        if step < 3:
            copies[step][seg].start()

    arrived(key_copy, 1, 0)
    arrived(key_copy, 1, 1)
    value_copy[0][1].start()
    own_tile(1, 0, False, True, True)
    own_tile(0, 0, True, True, False)
    arrived(key_copy, 2, 0)
    arrived(key_copy, 2, 1)
    arrived(value_copy, 1, 0)
    stage_v(1)
    arrived(value_copy, 1, 1)
    stage_v(2)
    own_tile(1, 1, True, False, True)
    arrived(key_copy, 3, 0)
    arrived(key_copy, 3, 1)
    stage_v(3)
    for seg in range(2):
        pass_back(gv_copy, own_v, sent_v, got_v, 3, seg)
    arrived(value_copy, 2, 0)
    arrived(value_copy, 2, 1)
    stage_k(1)()
    for seg in range(2):
        pass_back(gv_copy, own_v, sent_v, got_v, 2, seg)
    stage_k(2)()
    arrived(value_copy, 3, 0)
    arrived(value_copy, 3, 1)
    rest = stage_k(3)
    for seg in range(2):
        pass_back(gk_copy, own_k, sent_k, got_k, 3, seg)
    for seg in range(2):
        pass_back(gv_copy, own_v, sent_v, got_v, 1, seg)
    rest()
    for h in range(HEADS):
        for sg in range(2):
            dq_out[sg * SEG : (sg + 1) * SEG, h * DIM : (h + 1) * DIM] = (
                dq_acc[sg, h * SEG : (h + 1) * SEG, :] * FACTOR
            ).astype(jnp.bfloat16)
    store = pltpu.make_async_copy(dq_out, dq_hbm, out_sem)
    store.start()
    for seg in range(2):
        pass_back(gk_copy, own_k, sent_k, got_k, 2, seg)
    for seg in range(2):
        finish(gv_copy, own_v, got_v, seg, None, dv_ref)
    for seg in range(2):
        pass_back(gk_copy, own_k, sent_k, got_k, 1, seg)
    for seg in range(2):
        finish(gk_copy, own_k, got_k, seg, FACTOR, dk_ref)
    store.wait()
    for copies in (key_copy, value_copy, gv_copy[1:], gk_copy[1:]):
        for pair in copies:
            for copy in pair:
                copy.wait_send()


def per_device(queries, keys, values, outputs, out_grad, log_sums, pair_of):
    ctx_count = lax.axis_size("ctx")
    bf16, f32 = jnp.bfloat16, jnp.float32
    vmem = pl.BlockSpec(memory_space=pltpu.VMEM)
    hbm = pl.BlockSpec(memory_space=pl.ANY)
    smem = pl.BlockSpec(memory_space=pltpu.SMEM)
    sems = pltpu.SemaphoreType.DMA((3, 2))

    def body(*refs):
        kernel(ctx_count, *refs)

    return pl.pallas_call(
        body,
        out_shape=(
            jax.ShapeDtypeStruct(queries.shape, bf16),
            jax.ShapeDtypeStruct(keys.shape, f32),
            jax.ShapeDtypeStruct(values.shape, f32),
        ),
        in_specs=[smem, hbm, vmem, vmem, hbm, hbm, vmem],
        out_specs=(hbm, vmem, vmem),
        scratch_shapes=[
            pltpu.VMEM((2, SEG, HEADS * DIM), bf16),
            pltpu.VMEM((2, SEG, HEADS * DIM), bf16),
            pltpu.VMEM((2, SEG, HEADS * DIM), bf16),
            pltpu.VMEM((2, DIM, ROWS), bf16),
            pltpu.VMEM((2, DIM, ROWS), bf16),
            pltpu.VMEM((2, ROWS, DIM), f32),
            pltpu.VMEM((2, ROWS, DIM), f32),
        ]
        + [pltpu.VMEM((2, SEG, DIM), bf16)] * 6
        + [
            pltpu.VMEM((4, 2, ROWS, SEG), bf16),
            pltpu.VMEM((2, ROWS, SEG), bf16),
            pltpu.VMEM((2, ROWS, DIM), f32),
            pltpu.VMEM((2 * SEG, HEADS * DIM), bf16),
            pltpu.VMEM((4, 2, DIM, SEG), f32),
            pltpu.VMEM((4, 2, DIM, SEG), f32),
            pltpu.VMEM((3, 2, DIM, SEG), bf16),
            pltpu.VMEM((3, 2, DIM, SEG), bf16),
            pltpu.VMEM((3, 2, DIM, SEG), bf16),
            pltpu.VMEM((3, 2, DIM, SEG), bf16),
            pltpu.SemaphoreType.DMA((3, 2)),
            pltpu.SemaphoreType.DMA,
        ]
        + [sems] * 8,
        compiler_params=pltpu.CompilerParams(
            collective_id=0, has_side_effects=True, vmem_limit_bytes=56 * 2**20
        ),
        cost_estimate=pl.CostEstimate(
            flops=6_000_000_000, bytes_accessed=5_000_000, transcendentals=4_700_000
        ),
        name="gqa_backward",
    )(pair_of, queries, keys, values, outputs, out_grad, log_sums)


def solution(mesh):
    return jax.shard_map(
        per_device,
        mesh=mesh,
        in_specs=(
            P("ctx", "grp"),
            P("ctx", "grp"),
            P("ctx", "grp"),
            P("ctx", "grp"),
            P("ctx", "grp"),
            P("grp", "ctx"),
            P(),
        ),
        out_specs=(P("ctx", "grp"), P("ctx", "grp"), P("ctx", "grp")),
        check_vma=False,
    )
```

profile of v0, /device:TPU:8, one launch (start us, length us, event | category | flops | bytes accessed | tf_op | source)
XLA Modules:
  0.0 52.1 jit_solution(10673734300274470450)
XLA Ops:
  0.6 47.4 %gqa_backward.1 = (bf16[512,1024]{1,0:T(8,128)(2,1)}, f32[512,128]{1,0:T(8,128)}, f32[512,128]{1,0:T(8,128)}) custom-call(s32[64]{0:T(128)} %refs_0_.1, bf16[512,1024]{1,0:T(8,128)(2,1)} %refs_1_.1, bf16[512,128]{1,0:T(8,128)(2,1)} %refs_2_.1, bf16[512,128]{1,0:T(8,128)(2,1)} %refs_3_.1, bf16[512,1024]{1,0:T(8,128)(2,1)} %refs_4_.1, ...), custom_call_target="tpu_custom_call" | custom-call | flops 6000000000 | bytes 5000000 | tf_op jit(solution)/shard_map/gqa_backward/pallas_call | solution.py:277
  48.0 0.0 copy-start.1
  48.0 2.3 %copy.13 = bf16[512,1024]{1,0:T(8,128)(2,1)} copy(bf16[512,1024]{1,0:T(8,128)(2,1)} %get-tuple-element.6) | data formatting | bytes 2097152
  50.3 0.0 copy-done.1
  50.3 0.0 copy-start
  50.3 0.7 %copy.14 = f32[512,128]{1,0:T(8,128)} copy(f32[512,128]{1,0:T(8,128)S(1)} %copy-done.1) | data formatting | bytes 524288
  51.0 0.3 copy-done
  51.4 0.7 %copy.15 = f32[512,128]{1,0:T(8,128)} copy(f32[512,128]{1,0:T(8,128)S(1)} %copy-done) | data formatting | bytes 524288
Async XLA Ops:
  48.0 2.3 %copy-start.1 = (f32[512,128]{1,0:T(8,128)S(1)}, f32[512,128]{1,0:T(8,128)}, u32[]{:S(2)}) copy-start(f32[512,128]{1,0:T(8,128)} %get-tuple-element.7) | copy-start | bytes 786436
  50.3 1.0 %copy-start = (f32[512,128]{1,0:T(8,128)S(1)}, f32[512,128]{1,0:T(8,128)}, u32[]{:S(2)}) copy-start(f32[512,128]{1,0:T(8,128)} %get-tuple-element.8) | copy-start | bytes 786436
where the time goes:
time: 52.2 us; the launch traced here: 52.1 us
  Pallas kernels  47.4 us (91%)
  local copies, waits for them, and re-layouts  4.05 us (8%)
  between operations  0.65 us (1%)
    pallas_call x1, Pallas kernels, per_device(): pl.pallas_call(body, out_shape=(jax.ShapeDtypeStruct(queries.shape, bf16)...  47.4 us
    unnamed x7, local copies, waits for them, and re-layouts  4.05 us

commit v1 on v0

--- a/solution.py
+++ b/solution.py
@@ -24,14 +24,14 @@
 
 def kernel(
     ctx_count,
-    pair_ref, q_hbm, k_ref, v_ref, o_hbm, g_hbm, lse_ref,
-    dq_hbm, dk_ref, dv_ref,
-    q_in, g_in, o_in,
+    pair_hbm, q_hbm, k_hbm, v_hbm, o_hbm, g_hbm, lse_hbm,
+    dq_ref, dk_ref, dv_ref,
+    pair_ref, k_ref, v_ref, lse_ref, q_in, g_in, o_in,
     q_t, g_t, lse_b, delta_b,
     k1, k2, k3, v1, v2, v3,
     probs, dsc,
-    dq_acc, dq_out, own_v, own_k, sent_v, sent_k, got_v, got_k,
-    in_sem, out_sem,
+    dq_acc, own_v, own_k, sent_v, sent_k, got_v, got_k,
+    in_sem, small_sem,
     k_send, k_recv, v_send, v_recv, gv_send, gv_recv, gk_send, gk_recv,
 ):
     me = lax.axis_index("ctx")
@@ -48,6 +48,10 @@
             load = pltpu.make_async_copy(src.at[pl.ds(sg * SEG, SEG)], dst.at[sg], in_sem.at[i, sg])
             load.start()
             loads.append(load)
+    for i, (src, dst) in enumerate(((pair_hbm, pair_ref), (k_hbm, k_ref), (v_hbm, v_ref), (lse_hbm, lse_ref))):
+        load = pltpu.make_async_copy(src, dst, small_sem.at[i])
+        load.start()
+        loads.append(load)
 
     keys = [None, k1, k2, k3]
     values = [None, v1, v2, v3]
@@ -63,8 +67,8 @@
             device_id_type=MESH,
         )
 
-    key_copy = [[forward(keys, k_ref, s, g, k_send, k_recv) for g in range(2)] for s in range(3)]
-    value_copy = [[forward(values, v_ref, s, g, v_send, v_recv) for g in range(2)] for s in range(3)]
+    key_copy = [[forward(keys, k_hbm, s, g, k_send, k_recv) for g in range(2)] for s in range(3)]
+    value_copy = [[forward(values, v_hbm, s, g, v_send, v_recv) for g in range(2)] for s in range(3)]
 
     def back(sent, got, step, seg, send, recv):
         return pltpu.make_async_remote_copy(
@@ -80,27 +84,26 @@
     gk_copy = [None] + [[back(sent_k, got_k, s, g, gk_send, gk_recv) for g in range(2)] for s in (1, 2, 3)]
 
     pl.semaphore_wait(barrier, 2)
-    key_copy[0][0].start()
-    key_copy[0][1].start()
-    value_copy[0][0].start()
-
-    for load in loads:
-        load.wait()
-    for h in range(HEADS):
-        cols = slice(h * DIM, (h + 1) * DIM)
-        for sg in range(2):
-            qh = q_in[sg, :, cols]
-            gh = g_in[sg, :, cols]
-            q_t[sg, :, h * SEG : (h + 1) * SEG] = qh.T
-            g_t[sg, :, h * SEG : (h + 1) * SEG] = gh.T
-            delta = jnp.sum(
-                gh.astype(jnp.float32) * o_in[sg, :, cols].astype(jnp.float32), axis=1, keepdims=True
-            )
-            delta_b[sg, h * SEG : (h + 1) * SEG, :] = jnp.broadcast_to(delta, (SEG, DIM))
-            for j in range(SEG // DIM):
-                at = sg * SEG + j * DIM
-                row = lse_ref[h : h + 1, at : at + DIM] * LOG2E
-                lse_b[sg, h * SEG + j * DIM : h * SEG + (j + 1) * DIM, :] = jnp.broadcast_to(row, (DIM, DIM)).T
+
+    def prologue():
+        for load in loads:
+            load.wait()
+        for h in range(HEADS):
+            cols = slice(h * DIM, (h + 1) * DIM)
+            for sg in range(2):
+                qh = q_in[sg, :, cols]
+                gh = g_in[sg, :, cols]
+                q_t[sg, :, h * SEG : (h + 1) * SEG] = qh.T
+                g_t[sg, :, h * SEG : (h + 1) * SEG] = gh.T
+                delta = jnp.sum(
+                    gh.astype(jnp.float32) * o_in[sg, :, cols].astype(jnp.float32), axis=1, keepdims=True
+                )
+                delta_b[sg, h * SEG : (h + 1) * SEG, :] = jnp.broadcast_to(delta, (SEG, DIM))
+                for j in range(SEG // DIM):
+                    at = sg * SEG + j * DIM
+                    row = lse_ref[h : h + 1, at : at + DIM] * LOG2E
+                    lse_b[sg, h * SEG + j * DIM : h * SEG + (j + 1) * DIM, :] = jnp.broadcast_to(row, (DIM, DIM)).T
+        dq_acc[...] = jnp.zeros_like(dq_acc)
 
     def wide(x):
         return jnp.concatenate([x, x], axis=1)
@@ -131,11 +134,13 @@
     def g_heads(q_seg, h):
         return g_in[q_seg, :, h * DIM : (h + 1) * DIM]
 
-    def own_tile(q_seg, k_seg, diagonal, first_q, first_k):
+    def own_probs(q_seg, k_seg, diagonal):
+        probs_of(q_seg, k_ref[k_seg * SEG : (k_seg + 1) * SEG, :], probs.at[0, 0], diagonal)
+
+    def own_rest(q_seg, k_seg, first_k):
         key = k_ref[k_seg * SEG : (k_seg + 1) * SEG, :]
         value = v_ref[k_seg * SEG : (k_seg + 1) * SEG, :]
         p, d = probs.at[0, 0], dsc.at[0]
-        probs_of(q_seg, key, p, diagonal)
         dscores_of(q_seg, value, p, d)
         part_v = dot_nn(g_t[q_seg], p[...])
         part_k = dot_nn(q_t[q_seg], d[...])
@@ -146,15 +151,7 @@
         else:
             own_v[0, k_seg] += part_v
             own_k[0, k_seg] += part_k
-        if first_q:
-            dq_acc[q_seg] = part_q
-        else:
-            dq_acc[q_seg] += part_q
-
-    mine = pair_ref[me]
-    b_seg = [None] + [
-        lax.div(pair_ref[lax.rem(me + ctx_count - s, ctx_count)] - mine + ctx_count, ctx_count) for s in (1, 2, 3)
-    ]
+        dq_acc[q_seg] += part_q
 
     def pick(step, earlier, later):
         return jnp.where(jnp.broadcast_to(b_seg[step], earlier.shape) == 0, earlier, later)
@@ -174,21 +171,25 @@
 
     def stage_k(s):
         qb = b_seg[s]
-        key_a = keys[s][0]
-        key_b = pick(s, key_a, keys[s][1])
         value_a = values[s][0]
         value_b = pick(s, value_a, values[s][1])
         dscores_of(1, value_a, probs.at[s, 0], dsc.at[0])
         dscores_of(qb, value_b, probs.at[s, 1], dsc.at[1])
         spread(own_k, s, dot_nn(q_t[1], dsc[0]), dot_nn(q_t[qb], dsc[1]))
 
-        def rest():
-            part_b = dot_nn(dsc[1], key_b)
-            zero = jnp.zeros_like(part_b)
-            dq_acc[1] += dot_nn(dsc[0], key_a) + pick(s, zero, part_b)
-            dq_acc[0] += pick(s, part_b, zero)
-
-        return rest
+    def queries_of(s):
+        key_a = keys[s][0]
+        part_b = dot_nn(dsc[1], pick(s, key_a, keys[s][1]))
+        zero = jnp.zeros_like(part_b)
+        dq_acc[1] += dot_nn(dsc[0], key_a) + pick(s, zero, part_b)
+        dq_acc[0] += pick(s, part_b, zero)
+
+    def scaled_queries():
+        for h in range(HEADS):
+            for sg in range(2):
+                dq_ref[sg * SEG : (sg + 1) * SEG, h * DIM : (h + 1) * DIM] = (
+                    dq_acc[sg, h * SEG : (h + 1) * SEG, :] * FACTOR
+                ).astype(jnp.bfloat16)
 
     def pass_back(copies, own, sent, got, s, seg):
         total = own[s, seg]
@@ -210,53 +211,59 @@
         if step < 3:
             copies[step][seg].start()
 
+    key_copy[0][0].start()
+    key_copy[0][1].start()
+    value_copy[0][0].start()
+    prologue()
+    mine = pair_ref[me]
+    b_seg = [None] + [
+        lax.div(pair_ref[lax.rem(me + ctx_count - s, ctx_count)] - mine + ctx_count, ctx_count) for s in (1, 2, 3)
+    ]
     arrived(key_copy, 1, 0)
     arrived(key_copy, 1, 1)
+    own_probs(1, 0, False)
     value_copy[0][1].start()
-    own_tile(1, 0, False, True, True)
-    own_tile(0, 0, True, True, False)
     arrived(key_copy, 2, 0)
     arrived(key_copy, 2, 1)
     arrived(value_copy, 1, 0)
-    stage_v(1)
     arrived(value_copy, 1, 1)
     stage_v(2)
-    own_tile(1, 1, True, False, True)
     arrived(key_copy, 3, 0)
+    stage_v(1)
     arrived(key_copy, 3, 1)
     stage_v(3)
-    for seg in range(2):
-        pass_back(gv_copy, own_v, sent_v, got_v, 3, seg)
     arrived(value_copy, 2, 0)
+    pass_back(gv_copy, own_v, sent_v, got_v, 3, 0)
+    own_rest(1, 0, True)
+    pass_back(gv_copy, own_v, sent_v, got_v, 3, 1)
     arrived(value_copy, 2, 1)
-    stage_k(1)()
-    for seg in range(2):
-        pass_back(gv_copy, own_v, sent_v, got_v, 2, seg)
-    stage_k(2)()
+    stage_k(1)
+    pass_back(gv_copy, own_v, sent_v, got_v, 2, 0)
     arrived(value_copy, 3, 0)
+    queries_of(1)
+    own_probs(0, 0, True)
+    pass_back(gv_copy, own_v, sent_v, got_v, 2, 1)
     arrived(value_copy, 3, 1)
-    rest = stage_k(3)
-    for seg in range(2):
-        pass_back(gk_copy, own_k, sent_k, got_k, 3, seg)
-    for seg in range(2):
-        pass_back(gv_copy, own_v, sent_v, got_v, 1, seg)
-    rest()
-    for h in range(HEADS):
-        for sg in range(2):
-            dq_out[sg * SEG : (sg + 1) * SEG, h * DIM : (h + 1) * DIM] = (
-                dq_acc[sg, h * SEG : (h + 1) * SEG, :] * FACTOR
-            ).astype(jnp.bfloat16)
-    store = pltpu.make_async_copy(dq_out, dq_hbm, out_sem)
-    store.start()
-    for seg in range(2):
-        pass_back(gk_copy, own_k, sent_k, got_k, 2, seg)
-    for seg in range(2):
-        finish(gv_copy, own_v, got_v, seg, None, dv_ref)
-    for seg in range(2):
-        pass_back(gk_copy, own_k, sent_k, got_k, 1, seg)
-    for seg in range(2):
-        finish(gk_copy, own_k, got_k, seg, FACTOR, dk_ref)
-    store.wait()
+    stage_k(3)
+    pass_back(gk_copy, own_k, sent_k, got_k, 3, 0)
+    pass_back(gk_copy, own_k, sent_k, got_k, 3, 1)
+    queries_of(3)
+    pass_back(gv_copy, own_v, sent_v, got_v, 1, 0)
+    own_rest(0, 0, False)
+    stage_k(2)
+    pass_back(gk_copy, own_k, sent_k, got_k, 2, 0)
+    queries_of(2)
+    pass_back(gk_copy, own_k, sent_k, got_k, 2, 1)
+    pass_back(gv_copy, own_v, sent_v, got_v, 1, 1)
+    own_probs(1, 1, True)
+    pass_back(gk_copy, own_k, sent_k, got_k, 1, 0)
+    finish(gv_copy, own_v, got_v, 0, None, dv_ref)
+    pass_back(gk_copy, own_k, sent_k, got_k, 1, 1)
+    own_rest(1, 1, True)
+    finish(gv_copy, own_v, got_v, 1, None, dv_ref)
+    finish(gk_copy, own_k, got_k, 0, FACTOR, dk_ref)
+    scaled_queries()
+    finish(gk_copy, own_k, got_k, 1, FACTOR, dk_ref)
     for copies in (key_copy, value_copy, gv_copy[1:], gk_copy[1:]):
         for pair in copies:
             for copy in pair:
@@ -267,23 +274,26 @@
     ctx_count = lax.axis_size("ctx")
     bf16, f32 = jnp.bfloat16, jnp.float32
     vmem = pl.BlockSpec(memory_space=pltpu.VMEM)
-    hbm = pl.BlockSpec(memory_space=pl.ANY)
-    smem = pl.BlockSpec(memory_space=pltpu.SMEM)
+    hbm = pl.BlockSpec(memory_space=pltpu.HBM)
     sems = pltpu.SemaphoreType.DMA((3, 2))
 
     def body(*refs):
         kernel(ctx_count, *refs)
 
-    return pl.pallas_call(
+    grads = pl.pallas_call(
         body,
         out_shape=(
             jax.ShapeDtypeStruct(queries.shape, bf16),
             jax.ShapeDtypeStruct(keys.shape, f32),
             jax.ShapeDtypeStruct(values.shape, f32),
         ),
-        in_specs=[smem, hbm, vmem, vmem, hbm, hbm, vmem],
-        out_specs=(hbm, vmem, vmem),
+        in_specs=[hbm] * 7,
+        out_specs=(vmem, vmem, vmem),
         scratch_shapes=[
+            pltpu.SMEM(pair_of.shape, jnp.int32),
+            pltpu.VMEM(keys.shape, bf16),
+            pltpu.VMEM(values.shape, bf16),
+            pltpu.VMEM(log_sums.shape, f32),
             pltpu.VMEM((2, SEG, HEADS * DIM), bf16),
             pltpu.VMEM((2, SEG, HEADS * DIM), bf16),
             pltpu.VMEM((2, SEG, HEADS * DIM), bf16),
@@ -297,7 +307,6 @@
             pltpu.VMEM((4, 2, ROWS, SEG), bf16),
             pltpu.VMEM((2, ROWS, SEG), bf16),
             pltpu.VMEM((2, ROWS, DIM), f32),
-            pltpu.VMEM((2 * SEG, HEADS * DIM), bf16),
             pltpu.VMEM((4, 2, DIM, SEG), f32),
             pltpu.VMEM((4, 2, DIM, SEG), f32),
             pltpu.VMEM((3, 2, DIM, SEG), bf16),
@@ -305,17 +314,37 @@
             pltpu.VMEM((3, 2, DIM, SEG), bf16),
             pltpu.VMEM((3, 2, DIM, SEG), bf16),
             pltpu.SemaphoreType.DMA((3, 2)),
-            pltpu.SemaphoreType.DMA,
+            pltpu.SemaphoreType.DMA((4,)),
         ]
         + [sems] * 8,
         compiler_params=pltpu.CompilerParams(
-            collective_id=0, has_side_effects=True, vmem_limit_bytes=56 * 2**20
+            collective_id=0, has_side_effects=True, vmem_limit_bytes=40 * 2**20
         ),
         cost_estimate=pl.CostEstimate(
             flops=6_000_000_000, bytes_accessed=5_000_000, transcendentals=4_700_000
         ),
         name="gqa_backward",
-    )(pair_of, queries, keys, values, outputs, out_grad, log_sums)
+    )(*(pltpu.with_memory_space_constraint(x, pltpu.HBM) for x in (pair_of, queries, keys, values, outputs, out_grad, log_sums)))
+
+    def written(dq_ref, dk_ref, dv_ref, dq_hbm, dk_hbm, dv_hbm, sem):
+        copies = [
+            pltpu.make_async_copy(src, dst, sem.at[i])
+            for i, (src, dst) in enumerate(((dq_ref, dq_hbm), (dk_ref, dk_hbm), (dv_ref, dv_hbm)))
+        ]
+        for copy in copies:
+            copy.start()
+        for copy in copies:
+            copy.wait()
+
+    return pl.pallas_call(
+        written,
+        out_shape=tuple(jax.ShapeDtypeStruct(x.shape, x.dtype) for x in grads),
+        in_specs=[vmem] * 3,
+        out_specs=(hbm,) * 3,
+        scratch_shapes=[pltpu.SemaphoreType.DMA((3,))],
+        compiler_params=pltpu.CompilerParams(vmem_limit_bytes=8 * 2**20),
+        name="written",
+    )(*grads)
 
 
 def solution(mesh):

time: 52.2 us -> 46.4 us (0.89)
  local copies, waits for them, and re-layouts: 4.05 us -> 0 us
  Pallas kernels: 47.4 us -> 45.2 us
    unnamed x7 -> x0, local copies, waits for them, and re-layouts: 4.05 us -> none
    pallas_call x1, Pallas kernels: 47.4 us -> 44 us  [per_device(): pl.pallas_call(body, out_shape=(jax.ShapeDtypeStruct(queries.shape, bf16)...]
    pallas_call x0 -> x1, Pallas kernels: none -> 1.16 us  [per_device(): pl.pallas_call(written, out_shape=tuple((jax.ShapeDtypeStruct(x.shape, x....]
where the time goes in v1:
time: 46.4 us; the launch traced here: 46 us
  Pallas kernels  45.2 us (97%)
  between operations  0.8 us (2%)
    pallas_call x1, Pallas kernels, per_device(): pl.pallas_call(body, out_shape=(jax.ShapeDtypeStruct(queries.shape, bf16)...  44 us
    pallas_call x1, Pallas kernels, per_device(): pl.pallas_call(written, out_shape=tuple((jax.ShapeDtypeStruct(x.shape, x....  1.16 us

profile of v1, /device:TPU:8, one launch (start us, length us, event | category | flops | bytes accessed | tf_op | source)
XLA Modules:
  0.0 46.0 jit_solution(15035299705430677828)
XLA Ops:
  0.6 44.0 %gqa_backward.1 = (bf16[512,1024]{1,0:T(8,128)(2,1)S(1)}, f32[512,128]{1,0:T(8,128)S(1)}, f32[512,128]{1,0:T(8,128)S(1)}) custom-call(s32[64]{0:T(128)} %refs_0_.1, bf16[512,1024]{1,0:T(8,128)(2,1)} %refs_1_.1, bf16[512,128]{1,0:T(8,128)(2,1)} %refs_2_.1, bf16[512,128]{1,0:T(8,128)(2,1)} %refs_3_.1, bf16[512,1024]{1,0:T(8,128)(2,1)} %refs_4_.1, ...), custom_call_target="tpu_custom_call" | custom-call | flops 6000000000 | bytes 5000000 | tf_op jit(solution)/shard_map/gqa_backward/pallas_call | solution.py:283
  44.7 1.2 %written.1 = (bf16[512,1024]{1,0:T(8,128)(2,1)}, f32[512,128]{1,0:T(8,128)}, f32[512,128]{1,0:T(8,128)}) custom-call(bf16[512,1024]{1,0:T(8,128)(2,1)S(1)} %get-tuple-element.6.dq_ref, f32[512,128]{1,0:T(8,128)S(1)} %get-tuple-element.7.dk_ref, f32[512,128]{1,0:T(8,128)S(1)} %get-tuple-element.8.dv_ref), custom_call_target="tpu_custom_call" | custom-call | tf_op jit(solution)/shard_map/written/pallas_call | solution.py:339

commit v2 on v1

--- a/solution.py
+++ b/solution.py
@@ -8,6 +8,7 @@
 MESH = pl.DeviceIdType.MESH
 LOG2E = 1.4426950408889634
 SEG = 256
+HALF = 128
 HEADS = 8
 DIM = 128
 ROWS = HEADS * SEG
@@ -31,7 +32,7 @@
     k1, k2, k3, v1, v2, v3,
     probs, dsc,
     dq_acc, own_v, own_k, sent_v, sent_k, got_v, got_k,
-    in_sem, small_sem,
+    in_sem, small_sem, ready,
     k_send, k_recv, v_send, v_recv, gv_send, gv_recv, gk_send, gk_recv,
 ):
     me = lax.axis_index("ctx")
@@ -39,8 +40,7 @@
     left = lax.rem(me + ctx_count - 1, ctx_count)
 
     barrier = pltpu.get_barrier_semaphore()
-    for peer in (left, right):
-        pl.semaphore_signal(barrier, inc=1, device_id={"ctx": peer}, device_id_type=MESH)
+    pl.semaphore_signal(barrier, inc=1, device_id={"ctx": left}, device_id_type=MESH)
 
     loads = []
     for i, (src, dst) in enumerate(((q_hbm, q_in), (g_hbm, g_in), (o_hbm, o_in))):
@@ -57,10 +57,10 @@
     values = [None, v1, v2, v3]
 
     def forward(bufs, first, step, seg, send, recv):
-        src = first.at[pl.ds(seg * SEG, SEG)] if step == 0 else bufs[step].at[seg]
+        src = first if step == 0 else bufs[step]
         return pltpu.make_async_remote_copy(
-            src_ref=src,
-            dst_ref=bufs[step + 1].at[seg],
+            src_ref=src.at[:, seg],
+            dst_ref=bufs[step + 1].at[:, seg],
             send_sem=send.at[step, seg],
             recv_sem=recv.at[step, seg],
             device_id={"ctx": right},
@@ -83,7 +83,7 @@
     gv_copy = [None] + [[back(sent_v, got_v, s, g, gv_send, gv_recv) for g in range(2)] for s in (1, 2, 3)]
     gk_copy = [None] + [[back(sent_k, got_k, s, g, gk_send, gk_recv) for g in range(2)] for s in (1, 2, 3)]
 
-    pl.semaphore_wait(barrier, 2)
+    pl.semaphore_wait(barrier, 1)
 
     def prologue():
         for load in loads:
@@ -105,14 +105,14 @@
                     lse_b[sg, h * SEG + j * DIM : h * SEG + (j + 1) * DIM, :] = jnp.broadcast_to(row, (DIM, DIM)).T
         dq_acc[...] = jnp.zeros_like(dq_acc)
 
-    def wide(x):
-        return jnp.concatenate([x, x], axis=1)
+    def wide(x, width):
+        return jnp.concatenate([x] * (width // DIM), axis=1)
 
     def probs_of(q_seg, key, out, diagonal):
+        width = key.shape[0]
         for h in range(HEADS):
             rows = pl.ds(h * SEG, SEG)
-            qh = q_heads(q_seg, h)
-            x = dot_nt(qh, key) * (FACTOR * LOG2E) - wide(lse_b[q_seg, rows, :])
+            x = dot_nt(q_heads(q_seg, h), key) * (FACTOR * LOG2E) - wide(lse_b[q_seg, rows, :], width)
             p = jnp.exp2(x)
             if diagonal:
                 below = lax.broadcasted_iota(jnp.int32, (SEG, SEG), 1) <= lax.broadcasted_iota(
@@ -125,7 +125,7 @@
         for h in range(HEADS):
             rows = pl.ds(h * SEG, SEG)
             dp = dot_nt(g_heads(q_seg, h), value)
-            ds = pin[rows, :].astype(jnp.float32) * (dp - wide(delta_b[q_seg, rows, :]))
+            ds = pin[rows, :].astype(jnp.float32) * (dp - wide(delta_b[q_seg, rows, :], value.shape[0]))
             out[rows, :] = ds.astype(jnp.bfloat16)
 
     def q_heads(q_seg, h):
@@ -134,52 +134,58 @@
     def g_heads(q_seg, h):
         return g_in[q_seg, :, h * DIM : (h + 1) * DIM]
 
+    def segment(ref, seg, part=None):
+        return ref[seg].reshape(SEG, DIM) if part is None else ref[seg, part]
+
+    def add_own(own, seg, total, first):
+        for part in range(2):
+            cols = total[:, part * HALF : (part + 1) * HALF]
+            own[0, part, seg] = cols if first else own[0, part, seg] + cols
+
     def own_probs(q_seg, k_seg, diagonal):
-        probs_of(q_seg, k_ref[k_seg * SEG : (k_seg + 1) * SEG, :], probs.at[0, 0], diagonal)
+        probs_of(q_seg, segment(k_ref, k_seg), probs.at[0, 0], diagonal)
 
     def own_rest(q_seg, k_seg, first_k):
-        key = k_ref[k_seg * SEG : (k_seg + 1) * SEG, :]
-        value = v_ref[k_seg * SEG : (k_seg + 1) * SEG, :]
         p, d = probs.at[0, 0], dsc.at[0]
-        dscores_of(q_seg, value, p, d)
-        part_v = dot_nn(g_t[q_seg], p[...])
-        part_k = dot_nn(q_t[q_seg], d[...])
-        part_q = dot_nn(d[...], key)
-        if first_k:
-            own_v[0, k_seg] = part_v
-            own_k[0, k_seg] = part_k
-        else:
-            own_v[0, k_seg] += part_v
-            own_k[0, k_seg] += part_k
-        dq_acc[q_seg] += part_q
+        dscores_of(q_seg, segment(v_ref, k_seg), p, d)
+        add_own(own_v, k_seg, dot_nn(g_t[q_seg], p[...]), first_k)
+        add_own(own_k, k_seg, dot_nn(q_t[q_seg], d[...]), first_k)
+        dq_acc[q_seg] += dot_nn(d[...], segment(k_ref, k_seg))
 
     def pick(step, earlier, later):
         return jnp.where(jnp.broadcast_to(b_seg[step], earlier.shape) == 0, earlier, later)
 
-    def spread(own, step, part_a, part_b):
+    def spread(own, step, part, part_a, part_b):
         zero = jnp.zeros_like(part_b)
-        own[step, 0] = part_a + pick(step, part_b, zero)
-        own[step, 1] = pick(step, zero, part_b)
-
-    def stage_v(s):
-        qb = b_seg[s]
-        key_a = keys[s][0]
-        key_b = pick(s, key_a, keys[s][1])
-        probs_of(1, key_a, probs.at[s, 0], False)
-        probs_of(qb, key_b, probs.at[s, 1], False)
-        spread(own_v, s, dot_nn(g_t[1], probs[s, 0]), dot_nn(g_t[qb], probs[s, 1]))
-
-    def stage_k(s):
-        qb = b_seg[s]
-        value_a = values[s][0]
-        value_b = pick(s, value_a, values[s][1])
-        dscores_of(1, value_a, probs.at[s, 0], dsc.at[0])
-        dscores_of(qb, value_b, probs.at[s, 1], dsc.at[1])
-        spread(own_k, s, dot_nn(q_t[1], dsc[0]), dot_nn(q_t[qb], dsc[1]))
+        early = part_a + pick(step, part_b, zero)
+        late = pick(step, zero, part_b)
+        for p in (0, 1) if part is None else (part,):
+            cols = slice(p * HALF, (p + 1) * HALF) if part is None else slice(0, HALF)
+            own[step, p, 0] = early[:, cols]
+            own[step, p, 1] = late[:, cols]
+
+    def columns(part):
+        return slice(None) if part is None else pl.ds(part * HALF, HALF)
+
+    def stage_v(s, part):
+        qb, at = b_seg[s], columns(part)
+        key_a = segment(keys[s], 0, part)
+        key_b = pick(s, key_a, segment(keys[s], 1, part))
+        probs_of(1, key_a, probs.at[s, 0, :, at], False)
+        probs_of(qb, key_b, probs.at[s, 1, :, at], False)
+        spread(own_v, s, part, dot_nn(g_t[1], probs[s, 0, :, at]), dot_nn(g_t[qb], probs[s, 1, :, at]))
+
+    def stage_k(s, part):
+        qb, at = b_seg[s], columns(part)
+        value_a = segment(values[s], 0, part)
+        value_b = pick(s, value_a, segment(values[s], 1, part))
+        dscores_of(1, value_a, probs.at[s, 0, :, at], dsc.at[0, :, at])
+        dscores_of(qb, value_b, probs.at[s, 1, :, at], dsc.at[1, :, at])
+        spread(own_k, s, part, dot_nn(q_t[1], dsc[0, :, at]), dot_nn(q_t[qb], dsc[1, :, at]))
 
     def queries_of(s):
-        key_a = keys[s][0]
-        part_b = dot_nn(dsc[1], pick(s, key_a, keys[s][1]))
+        key_a = segment(keys[s], 0)
+        part_b = dot_nn(dsc[1], pick(s, key_a, segment(keys[s], 1)))
         zero = jnp.zeros_like(part_b)
         dq_acc[1] += dot_nn(dsc[0], key_a) + pick(s, zero, part_b)
         dq_acc[0] += pick(s, part_b, zero)
@@ -204,7 +210,9 @@
         total = own[0, seg] + got[0, seg].astype(jnp.float32)
         if scale is not None:
             total = total * scale
-        out[seg * SEG : (seg + 1) * SEG, :] = total.T
+        for half in range(2):
+            at = half * SEG + seg * HALF
+            out[at : at + HALF, :] = total[half].T
 
     def arrived(copies, step, seg):
         copies[step - 1][seg].wait_recv()
@@ -214,6 +222,7 @@
     key_copy[0][0].start()
     key_copy[0][1].start()
     value_copy[0][0].start()
+    pl.semaphore_signal(ready, inc=1, device_id={"ctx": right}, device_id_type=MESH)
     prologue()
     mine = pair_ref[me]
     b_seg = [None] + [
@@ -221,48 +230,51 @@
     ]
     arrived(key_copy, 1, 0)
     arrived(key_copy, 1, 1)
+    value_copy[0][1].start()
     own_probs(1, 0, False)
-    value_copy[0][1].start()
+    own_rest(1, 0, True)
+    own_probs(0, 0, True)
     arrived(key_copy, 2, 0)
+    own_rest(0, 0, False)
     arrived(key_copy, 2, 1)
     arrived(value_copy, 1, 0)
     arrived(value_copy, 1, 1)
-    stage_v(2)
+    stage_v(2, None)
     arrived(key_copy, 3, 0)
-    stage_v(1)
+    stage_v(3, 0)
+    pl.semaphore_wait(ready, 1)
+    pass_back(gv_copy, own_v, sent_v, got_v, 3, 0)
+    own_probs(1, 1, True)
     arrived(key_copy, 3, 1)
-    stage_v(3)
+    stage_v(3, 1)
+    pass_back(gv_copy, own_v, sent_v, got_v, 3, 1)
     arrived(value_copy, 2, 0)
-    pass_back(gv_copy, own_v, sent_v, got_v, 3, 0)
-    own_rest(1, 0, True)
-    pass_back(gv_copy, own_v, sent_v, got_v, 3, 1)
+    stage_v(1, None)
     arrived(value_copy, 2, 1)
-    stage_k(1)
     pass_back(gv_copy, own_v, sent_v, got_v, 2, 0)
+    pass_back(gv_copy, own_v, sent_v, got_v, 2, 1)
     arrived(value_copy, 3, 0)
-    queries_of(1)
-    own_probs(0, 0, True)
-    pass_back(gv_copy, own_v, sent_v, got_v, 2, 1)
+    stage_k(3, 0)
+    pass_back(gk_copy, own_k, sent_k, got_k, 3, 0)
     arrived(value_copy, 3, 1)
-    stage_k(3)
-    pass_back(gk_copy, own_k, sent_k, got_k, 3, 0)
+    stage_k(3, 1)
     pass_back(gk_copy, own_k, sent_k, got_k, 3, 1)
     queries_of(3)
     pass_back(gv_copy, own_v, sent_v, got_v, 1, 0)
-    own_rest(0, 0, False)
-    stage_k(2)
+    stage_k(2, None)
     pass_back(gk_copy, own_k, sent_k, got_k, 2, 0)
     queries_of(2)
     pass_back(gk_copy, own_k, sent_k, got_k, 2, 1)
+    own_rest(1, 1, True)
     pass_back(gv_copy, own_v, sent_v, got_v, 1, 1)
-    own_probs(1, 1, True)
+    stage_k(1, None)
     pass_back(gk_copy, own_k, sent_k, got_k, 1, 0)
+    pass_back(gk_copy, own_k, sent_k, got_k, 1, 1)
     finish(gv_copy, own_v, got_v, 0, None, dv_ref)
-    pass_back(gk_copy, own_k, sent_k, got_k, 1, 1)
-    own_rest(1, 1, True)
     finish(gv_copy, own_v, got_v, 1, None, dv_ref)
+    queries_of(1)
+    scaled_queries()
     finish(gk_copy, own_k, got_k, 0, FACTOR, dk_ref)
-    scaled_queries()
     finish(gk_copy, own_k, got_k, 1, FACTOR, dk_ref)
     for copies in (key_copy, value_copy, gv_copy[1:], gk_copy[1:]):
         for pair in copies:
@@ -276,6 +288,9 @@
     vmem = pl.BlockSpec(memory_space=pltpu.VMEM)
     hbm = pl.BlockSpec(memory_space=pltpu.HBM)
     sems = pltpu.SemaphoreType.DMA((3, 2))
+
+    blocks = (2, 2, HALF, DIM)
+    operands = (pair_of, queries, keys.reshape(blocks), values.reshape(blocks), outputs, out_grad, log_sums)
 
     def body(*refs):
         kernel(ctx_count, *refs)
@@ -291,8 +306,8 @@
         out_specs=(vmem, vmem, vmem),
         scratch_shapes=[
             pltpu.SMEM(pair_of.shape, jnp.int32),
-            pltpu.VMEM(keys.shape, bf16),
-            pltpu.VMEM(values.shape, bf16),
+            pltpu.VMEM((2, 2, HALF, DIM), bf16),
+            pltpu.VMEM((2, 2, HALF, DIM), bf16),
             pltpu.VMEM(log_sums.shape, f32),
             pltpu.VMEM((2, SEG, HEADS * DIM), bf16),
             pltpu.VMEM((2, SEG, HEADS * DIM), bf16),
@@ -302,19 +317,20 @@
             pltpu.VMEM((2, ROWS, DIM), f32),
             pltpu.VMEM((2, ROWS, DIM), f32),
         ]
-        + [pltpu.VMEM((2, SEG, DIM), bf16)] * 6
+        + [pltpu.VMEM((2, 2, HALF, DIM), bf16)] * 6
         + [
             pltpu.VMEM((4, 2, ROWS, SEG), bf16),
             pltpu.VMEM((2, ROWS, SEG), bf16),
             pltpu.VMEM((2, ROWS, DIM), f32),
-            pltpu.VMEM((4, 2, DIM, SEG), f32),
-            pltpu.VMEM((4, 2, DIM, SEG), f32),
-            pltpu.VMEM((3, 2, DIM, SEG), bf16),
-            pltpu.VMEM((3, 2, DIM, SEG), bf16),
-            pltpu.VMEM((3, 2, DIM, SEG), bf16),
-            pltpu.VMEM((3, 2, DIM, SEG), bf16),
+            pltpu.VMEM((4, 2, 2, DIM, HALF), f32),
+            pltpu.VMEM((4, 2, 2, DIM, HALF), f32),
+            pltpu.VMEM((3, 2, 2, DIM, HALF), bf16),
+            pltpu.VMEM((3, 2, 2, DIM, HALF), bf16),
+            pltpu.VMEM((3, 2, 2, DIM, HALF), bf16),
+            pltpu.VMEM((3, 2, 2, DIM, HALF), bf16),
             pltpu.SemaphoreType.DMA((3, 2)),
             pltpu.SemaphoreType.DMA((4,)),
+            pltpu.SemaphoreType.REGULAR,
         ]
         + [sems] * 8,
         compiler_params=pltpu.CompilerParams(
@@ -324,7 +340,7 @@
             flops=6_000_000_000, bytes_accessed=5_000_000, transcendentals=4_700_000
         ),
         name="gqa_backward",
-    )(*(pltpu.with_memory_space_constraint(x, pltpu.HBM) for x in (pair_of, queries, keys, values, outputs, out_grad, log_sums)))
+    )(*(pltpu.with_memory_space_constraint(x, pltpu.HBM) for x in operands))
 
     def written(dq_ref, dk_ref, dv_ref, dq_hbm, dk_hbm, dv_hbm, sem):
         copies = [

time: 46.4 us -> 43.4 us (0.935)
  Pallas kernels: 45.2 us -> 42.4 us
    pallas_call x1, Pallas kernels: 44 us -> 41.3 us  [per_device(): pl.pallas_call(body, out_shape=(jax.ShapeDtypeStruct(queries.shape, bf16)...]
where the time goes in v2:
time: 43.4 us; the launch traced here: 43.2 us
  Pallas kernels  42.4 us (98%)
  between operations  0.8 us (2%)
    pallas_call x1, Pallas kernels, per_device(): pl.pallas_call(body, out_shape=(jax.ShapeDtypeStruct(queries.shape, bf16)...  41.3 us
    pallas_call x1, Pallas kernels, per_device(): pl.pallas_call(written, out_shape=tuple((jax.ShapeDtypeStruct(x.shape, x....  1.16 us

profile of v2, /device:TPU:8, one launch (start us, length us, event | category | flops | bytes accessed | tf_op | source)
XLA Modules:
  0.0 43.2 jit_solution(11046400608941064770)
XLA Ops:
  0.6 41.3 %gqa_backward.1 = (bf16[512,1024]{1,0:T(8,128)(2,1)S(1)}, f32[512,128]{1,0:T(8,128)S(1)}, f32[512,128]{1,0:T(8,128)S(1)}) custom-call(s32[64]{0:T(128)} %refs_0_.1, bf16[512,1024]{1,0:T(8,128)(2,1)} %refs_1_.1, bf16[2,2,128,128]{3,2,1,0:T(8,128)(2,1)} %bitcast.2, bf16[2,2,128,128]{3,2,1,0:T(8,128)(2,1)} %bitcast.3, bf16[512,1024]{1,0:T(8,128)(2,1)} %refs_4_.1, ...), custom_call_target="tpu_custom_call" | custom-call | flops 6000000000 | bytes 5000000 | tf_op jit(solution)/shard_map/gqa_backward/pallas_call | solution.py:298
  41.9 1.2 %written.1 = (bf16[512,1024]{1,0:T(8,128)(2,1)}, f32[512,128]{1,0:T(8,128)}, f32[512,128]{1,0:T(8,128)}) custom-call(bf16[512,1024]{1,0:T(8,128)(2,1)S(1)} %get-tuple-element.6.dq_ref, f32[512,128]{1,0:T(8,128)S(1)} %get-tuple-element.7.dk_ref, f32[512,128]{1,0:T(8,128)S(1)} %get-tuple-element.8.dv_ref), custom_call_target="tpu_custom_call" | custom-call | tf_op jit(solution)/shard_map/written/pallas_call | solution.py:355

commit v3 on v2

--- a/solution.py
+++ b/solution.py
@@ -244,7 +244,6 @@
     stage_v(3, 0)
     pl.semaphore_wait(ready, 1)
     pass_back(gv_copy, own_v, sent_v, got_v, 3, 0)
-    own_probs(1, 1, True)
     arrived(key_copy, 3, 1)
     stage_v(3, 1)
     pass_back(gv_copy, own_v, sent_v, got_v, 3, 1)
@@ -253,26 +252,27 @@
     arrived(value_copy, 2, 1)
     pass_back(gv_copy, own_v, sent_v, got_v, 2, 0)
     pass_back(gv_copy, own_v, sent_v, got_v, 2, 1)
+    own_probs(1, 1, True)
     arrived(value_copy, 3, 0)
     stage_k(3, 0)
     pass_back(gk_copy, own_k, sent_k, got_k, 3, 0)
     arrived(value_copy, 3, 1)
     stage_k(3, 1)
     pass_back(gk_copy, own_k, sent_k, got_k, 3, 1)
+    pass_back(gv_copy, own_v, sent_v, got_v, 1, 0)
     queries_of(3)
-    pass_back(gv_copy, own_v, sent_v, got_v, 1, 0)
     stage_k(2, None)
     pass_back(gk_copy, own_k, sent_k, got_k, 2, 0)
     queries_of(2)
     pass_back(gk_copy, own_k, sent_k, got_k, 2, 1)
+    pass_back(gv_copy, own_v, sent_v, got_v, 1, 1)
     own_rest(1, 1, True)
-    pass_back(gv_copy, own_v, sent_v, got_v, 1, 1)
     stage_k(1, None)
     pass_back(gk_copy, own_k, sent_k, got_k, 1, 0)
     pass_back(gk_copy, own_k, sent_k, got_k, 1, 1)
+    queries_of(1)
     finish(gv_copy, own_v, got_v, 0, None, dv_ref)
     finish(gv_copy, own_v, got_v, 1, None, dv_ref)
-    queries_of(1)
     scaled_queries()
     finish(gk_copy, own_k, got_k, 0, FACTOR, dk_ref)
     finish(gk_copy, own_k, got_k, 1, FACTOR, dk_ref)

time: 43.4 us -> 42.5 us (0.979)
  Pallas kernels: 42.4 us -> 41.6 us
    pallas_call x1, Pallas kernels: 41.3 us -> 40.4 us  [per_device(): pl.pallas_call(body, out_shape=(jax.ShapeDtypeStruct(queries.shape, bf16)...]
where the time goes in v3:
time: 42.5 us; the launch traced here: 42.4 us
  Pallas kernels  41.6 us (98%)
  between operations  0.8 us (2%)
    pallas_call x1, Pallas kernels, per_device(): pl.pallas_call(body, out_shape=(jax.ShapeDtypeStruct(queries.shape, bf16)...  40.4 us
    pallas_call x1, Pallas kernels, per_device(): pl.pallas_call(written, out_shape=tuple((jax.ShapeDtypeStruct(x.shape, x....  1.16 us

profile of v3, /device:TPU:8, one launch (start us, length us, event | category | flops | bytes accessed | tf_op | source)
XLA Modules:
  0.0 42.4 jit_solution(7166493511650750357)
XLA Ops:
  0.6 40.4 %gqa_backward.1 = (bf16[512,1024]{1,0:T(8,128)(2,1)S(1)}, f32[512,128]{1,0:T(8,128)S(1)}, f32[512,128]{1,0:T(8,128)S(1)}) custom-call(s32[64]{0:T(128)} %refs_0_.1, bf16[512,1024]{1,0:T(8,128)(2,1)} %refs_1_.1, bf16[2,2,128,128]{3,2,1,0:T(8,128)(2,1)} %bitcast.2, bf16[2,2,128,128]{3,2,1,0:T(8,128)(2,1)} %bitcast.3, bf16[512,1024]{1,0:T(8,128)(2,1)} %refs_4_.1, ...), custom_call_target="tpu_custom_call" | custom-call | flops 6000000000 | bytes 5000000 | tf_op jit(solution)/shard_map/gqa_backward/pallas_call | solution.py:298
  41.1 1.2 %written.1 = (bf16[512,1024]{1,0:T(8,128)(2,1)}, f32[512,128]{1,0:T(8,128)}, f32[512,128]{1,0:T(8,128)}) custom-call(bf16[512,1024]{1,0:T(8,128)(2,1)S(1)} %get-tuple-element.6.dq_ref, f32[512,128]{1,0:T(8,128)S(1)} %get-tuple-element.7.dk_ref, f32[512,128]{1,0:T(8,128)S(1)} %get-tuple-element.8.dv_ref), custom_call_target="tpu_custom_call" | custom-call | tf_op jit(solution)/shard_map/written/pallas_call | solution.py:355
